TPU v7x, 128 devices: a whole 4x4x4 slice. The times are simulated.
128 devices in a mesh: occ: 8 (over y, core), vir: 16 (over z, x).
Axes of the slice: x: 4, y: 4, z: 4, core: 2. Of those that a mesh axis runs over, the one named last changes fastest.
Arguments:
- amplitude: bfloat16 [16, 640, 8, 640], P(None, 'vir'), may hold values from -6 to 6
- integral: bfloat16 [8, 640, 16, 640], P(None, 'vir', 'occ'), may hold values from -0.25 to 0.25
- occ_irrep: int32 [16], replicated, may hold values from 0 to 7
- kocc_irrep: int32 [8], replicated, may hold values from 0 to 7
- vir_irrep: int32 [640], replicated, may hold values from 0 to 7, as said below
Outputs:
- residual: bfloat16 [16, 640, 16, 640], P(None, 'vir', 'occ')
Inputs may be any that keep to these rules, and one draw needn't show every extreme that they name: `occ_irrep`: D2h irrep labels. `kocc_irrep`: D2h irrep labels. D2h irrep labels, ordered by irrep: vir_irrep never falls along the virtuals. The eight irreps hold, in an order that differs from draw to draw, 160, 120, three times 2 * 40 and three times 640 // 16 virtuals, so at most 160 virtuals share one irrep, and one irrep holds exactly that many.
All inputs are finite; a program needn't handle non-finite values.
Results may differ from a plain program's by a relative error of at most 0.0051.
Values may be sent and summed in bfloat16 or wider, within the bound.
A program may use at most 128 MiB of HBM per device.

v0:
```python
import jax
import jax.numpy as jnp
from jax import lax
from jax.sharding import PartitionSpec as P


def shards(amplitude, integral, occ_irrep, kocc_irrep, vir_irrep):
    vir_pos = lax.axis_index("vir")
    occ_pos = lax.axis_index("occ")
    local_a = amplitude.shape[1]
    local_j = integral.shape[2]
    n_occ = lax.axis_size("occ")
    n_vir = lax.axis_size("vir")
    a_labels = lax.dynamic_slice_in_dim(vir_irrep, vir_pos * local_a, local_a)
    j_labels = lax.dynamic_slice_in_dim(occ_irrep, occ_pos * local_j, local_j)
    left = jnp.bitwise_xor(occ_irrep[:, None], a_labels[None, :])
    right = jnp.bitwise_xor(kocc_irrep[:, None], vir_irrep[None, :])
    tmask = left[:, :, None, None] == right[None, None, :, :]
    tsym = jnp.where(tmask, amplitude, jnp.zeros_like(amplitude))
    col_key = jnp.bitwise_xor(j_labels[:, None], vir_irrep[None, :])
    piece = lax.all_gather(integral, "vir", axis=1, tiled=True)
    row_key = jnp.bitwise_xor(kocc_irrep[:, None], vir_irrep[None, :])
    pmask = row_key[:, :, None, None] == col_key[None, None, :, :]
    masked = jnp.where(pmask, piece, jnp.zeros_like(piece))
    cycle = jnp.einsum("iakc,kcjb->iajb", tsym, masked, preferred_element_type=jnp.float32).astype(
        jnp.bfloat16
    )
    batch = cycle.shape[0]
    width = cycle.shape[3]
    packed = cycle.reshape(n_occ, local_j, local_a, local_j, n_vir, local_a)
    packed = jnp.transpose(packed, (0, 4, 1, 2, 3, 5)).reshape(
        n_occ * n_vir * local_j, local_a, local_j, local_a
    )
    moved = lax.all_to_all(packed, ("occ", "vir"), split_axis=0, concat_axis=0, tiled=True)
    moved = moved.reshape(n_occ, n_vir, local_j, local_a, local_j, local_a)
    mirror = jnp.transpose(moved, (0, 4, 5, 2, 1, 3)).reshape(batch, local_a, local_j, width)
    return (cycle.astype(jnp.float32) + mirror.astype(jnp.float32)).astype(jnp.bfloat16)


def solution(mesh):
    in_specs = (P(None, "vir", None, None), P(None, "vir", "occ", None), P(), P(), P())
    out_specs = P(None, "vir", "occ", None)
    return jax.shard_map(shards, mesh=mesh, in_specs=in_specs, out_specs=out_specs, check_vma=False)
```

profile of v0, /device:TPU:1, one launch (start us, length us, event | category | flops | bytes accessed | tf_op | source)
XLA Modules:
  0.0 248.0 jit_solution(1288182222363210847)
XLA Ops:
  6.5 0.0 all-gather.2.cloned.1.call-start
  6.5 0.7 all-gather.2.cloned.1.call-update
  7.3 0.7 dynamic_slice.7
  8.0 0.8 dynamic_slice.6
  8.8 0.7 broadcast_xor_fusion.1
  9.5 0.8 broadcast_xor_fusion.2
  10.2 0.8 broadcast_xor_fusion
  11.0 6.8 %fusion.3 = bf16[16,40,8,640,1]{3,2,1,0,4:T(8,128)(2,1)} fusion(bf16[16,40,8,640]{3,2,1,0:T(8,128)(2,1)} %param.5, s32[8,640]{1,0:T(8,128)S(1)} %broadcast_xor_fusion, s32[16,40]{1,0:T(8,128)S(1)} %broadcast_xor_fusion.1), kind=kLoop, calls=%fused_computation.6 | loop fusion | flops 6553600 | bytes 13130240 | tf_op jit(solution)/shard_map/jit(_where)/select_n | solution.py:19
  17.8 87.7 %all-gather.2.cloned.1.call-done = bf16[8,640,2,640]{3,2,1,0:T(2,128)(2,1)} async-done(((bf16[8,40,2,640]{3,2,1,0:T(2,128)(2,1)}), bf16[8,640,2,640]{3,2,1,0:T(2,128)(2,1)}) %all-gather.2.cloned.1.call-update) | async-done | bytes 13107216 | tf_op jit(solution)/shard_map/all_gather | solution.py:21
  105.5 24.8 %compare_select_fusion = bf16[8,640,2,640]{3,2,1,0:T(2,128)(2,1)S(1)} fusion(bf16[8,640,2,640]{3,2,1,0:T(2,128)(2,1)} %all-gather.2.cloned.1.call-done, s32[2,640]{1,0:T(2,128)S(1)} %broadcast_xor_fusion.2, s32[8,640]{1,0:T(8,128)S(1)} %broadcast_xor_fusion), kind=kLoop, calls=%fused_computation | loop fusion | flops 13107200 | bytes 26240000 | tf_op jit(solution)/shard_map/jit(_where)/select_n | solution.py:24
  130.3 12.1 %bitcast_convert_fusion = bf16[16,40,2,640]{3,1,2,0:T(8,128)(2,1)S(1)} fusion(bf16[8,640,2,640]{3,2,1,0:T(2,128)(2,1)S(1)} %compare_select_fusion, bf16[16,40,8,640,1]{3,2,1,0,4:T(8,128)(2,1)} %fusion.3), kind=kOutput, calls=%fused_computation.8 | convolution fusion | flops 8389427200 | bytes 21299200 | tf_op jit(solution)/shard_map/iakc,kcjb->iajb/dot_general | solution.py:25
  142.4 0.0 copy-start
  142.4 8.6 %reshape.114 = bf16[8,2,40,2,16,40]{5,4,2,3,1,0:T(8,128)(2,1)} reshape(bf16[16,40,2,640]{3,1,2,0:T(8,128)(2,1)S(1)} %bitcast_convert_fusion) | data formatting | bytes 3276800 | tf_op jit(solution)/shard_map/reshape | solution.py:30
  151.0 6.2 %copy.11 = bf16[8,2,40,2,16,40]{5,2,3,1,4,0:T(8,128)(2,1)} copy(bf16[8,2,40,2,16,40]{5,4,2,3,1,0:T(8,128)(2,1)} %reshape.114) | data formatting | bytes 3276800 | tf_op jit(solution)/shard_map/reshape | solution.py:30
  157.2 0.0 copy-done
  157.2 10.1 %reshape.121 = bf16[128,2,3200]{2,1,0:T(2,128)(2,1)S(1)} reshape(bf16[256,2,40,40]{3,2,1,0:T(8,128)(2,1)} %bitcast.27) | data formatting | bytes 3276800
  167.3 32.5 %all_to_all.5 = bf16[128,2,3200]{2,1,0:T(2,128)(2,1)S(1)} all-to-all(bf16[128,2,3200]{2,1,0:T(2,128)(2,1)S(1)} %reshape.121), channel_id=1, replica_groups=mesh['occ'=8,'vir'=16] {'occ','vir'}, dimensions={0} | all-to-all | bytes 3276800 | tf_op jit(solution)/shard_map/all_to_all | solution.py:34
  199.7 9.4 %reshape.122 = bf16[256,2,40,40]{3,2,1,0:T(8,128)(2,1)} reshape(bf16[128,2,3200]{2,1,0:T(2,128)(2,1)S(1)} %all_to_all.5) | data formatting | bytes 3276800
  209.2 7.9 %convert_bitcast_fusion = f32[8,2,40,2,16,40]{2,5,1,3,4,0:T(8,128)} fusion(bf16[8,16,2,40,2,40]{5,3,4,2,1,0:T(8,128)(2,1)} %bitcast.28), kind=kLoop, calls=%fused_computation.5 | loop fusion | flops 819200 | bytes 4915200 | tf_op jit(solution)/shard_map/convert_element_type | solution.py:37
  217.1 11.7 %copy.12 = f32[8,2,40,2,16,40]{5,4,2,3,1,0:T(8,128)} copy(f32[8,2,40,2,16,40]{2,5,1,3,4,0:T(8,128)} %convert_bitcast_fusion) | data formatting | bytes 6553600 | tf_op jit(solution)/shard_map/convert_element_type | solution.py:37
  228.8 8.2 %reshape.116 = f32[16,40,2,640]{3,1,2,0:T(8,128)S(1)} reshape(f32[8,2,40,2,16,40]{5,4,2,3,1,0:T(8,128)} %copy.12) | data formatting | bytes 6553600 | tf_op jit(solution)/shard_map/convert_element_type | solution.py:37
  237.0 1.8 add_convert_fusion
  238.8 2.4 copy.13
Async XLA Ops:
  6.5 99.0 %all-gather.2.cloned.1.call-start = ((), (), s32[]{:S(2)}) async-start(), calls=%async_computation.1 | async-start | bytes 13926400 | tf_op jit(solution)/shard_map/all_gather | solution.py:21
  142.4 14.8 %copy-start = (bf16[16,40,2,640]{3,1,2,0:T(8,128)(2,1)}, bf16[16,40,2,640]{3,1,2,0:T(8,128)(2,1)S(1)}, u32[]{:S(2)}) copy-start(bf16[16,40,2,640]{3,1,2,0:T(8,128)(2,1)S(1)} %bitcast_convert_fusion) | copy-start | bytes 4915204
Sparse Core Ops, SparseCore 0:
  9.6 95.9 all-gather.1
where the time goes:
time: 249 us; the launch traced here: 248 us
  waiting for transfers between devices  88.4 us (36%)
  local copies, waits for them, and re-layouts  58.1 us (23%)
  other arithmetic  43.5 us (17%)
  blocking collectives  32.5 us (13%)
  between operations  13.4 us (5%)
  matrix products  12.1 us (5%)
    all_gather x1, waiting for transfers between devices, shards(): piece = lax.all_gather(integral, 'vir', axis=1, tiled=True)  87.7 us
    all_to_all x1, blocking collectives, shards(): lax.all_to_all(packed, ('occ', 'vir'), split_axis=0, concat_axis=0, tiled...  32.5 us
    select_n x1, other arithmetic, shards(): masked = jnp.where(pmask, piece, jnp.zeros_like(piece))  24.8 us
    convert_element_type x2, local copies, waits for them, and re-layouts, shards(): mirror.astype(jnp.float32)  19.9 us
    unnamed x4, local copies, waits for them, and re-layouts  19.5 us
    reshape x2, local copies, waits for them, and re-layouts, shards(): packed = cycle.reshape(n_occ, local_j, local_a, local_j, n_vir, local_a)  14.8 us
    dot_general x1, matrix products, shards(): jnp.einsum('iakc,kcjb->iajb', tsym, masked, preferred_element_type=jnp.fl...  12.1 us
    convert_element_type x1, other arithmetic, shards(): mirror.astype(jnp.float32)  7.91 us
  transfers between devices with their start and end apart: 1, of which 1 were waited for; matrix products, arithmetic and copies ran while one was open for 4% of the time, Pallas kernels for 0%

commit v1 on v0

v1 whole, which is shorter than its diff:
```python
import jax
import jax.numpy as jnp
from jax import lax
from jax.sharding import PartitionSpec as P

WIN = 160


def shards(amplitude, integral, occ_irrep, kocc_irrep, vir_irrep):
    vir_pos = lax.axis_index("vir")
    occ_pos = lax.axis_index("occ")
    local_a = amplitude.shape[1]
    local_j = integral.shape[2]
    n_occ = lax.axis_size("occ")
    n_vir = lax.axis_size("vir")
    nv = vir_irrep.shape[0]
    own = lax.dynamic_slice_in_dim(vir_irrep, vir_pos * local_a, 1)[0]
    j_labels = lax.dynamic_slice_in_dim(occ_irrep, occ_pos * local_j, local_j)
    firsts = jnp.sum((vir_irrep[None, :] < jnp.arange(8)[:, None]).astype(jnp.int32), axis=1)
    firsts = jnp.minimum(firsts, nv - WIN)

    def select(labels):
        start = jnp.sum(
            jnp.where(labels[..., None] == jnp.arange(8), firsts, 0), axis=-1
        )
        b = jnp.arange(nv)[:, None]
        n = jnp.arange(WIN)[None, :]
        hit = (b == n + start[..., None, None]) & (vir_irrep[:, None] == labels[..., None, None])
        return hit.astype(jnp.bfloat16)

    wlab = kocc_irrep[:, None] ^ j_labels[None, :] ^ own
    packed = jnp.einsum(
        "kcjb,kjbn->kcjn", integral, select(wlab), preferred_element_type=jnp.float32
    ).astype(jnp.bfloat16)
    packed = packed.reshape(packed.shape[0], local_a, local_j * WIN)
    panels = lax.all_gather(packed, "vir", axis=1, tiled=True)
    left = occ_irrep ^ own
    right = kocc_irrep[:, None] ^ vir_irrep[None, :]
    tmask = left[:, None, None, None] == right[None, None, :, :]
    tsym = jnp.where(tmask, amplitude, jnp.zeros_like(amplitude))
    cyc = jnp.einsum("iakc,kcn->ian", tsym, panels, preferred_element_type=jnp.float32).astype(jnp.bfloat16)
    batch = cyc.shape[0]
    cyc = cyc.reshape(batch, local_a, local_j, WIN)
    clab = left[:, None] ^ j_labels[None, :]
    cycle = jnp.einsum(
        "iajn,ijbn->iajb", cyc, select(clab), preferred_element_type=jnp.float32
    ).astype(jnp.bfloat16)
    width = nv
    moved = cycle.reshape(n_occ, local_j, local_a, local_j, n_vir, local_a)
    moved = jnp.transpose(moved, (0, 4, 1, 2, 3, 5)).reshape(n_occ * n_vir * local_j, local_a, local_j, local_a)
    moved = lax.all_to_all(moved, ("occ", "vir"), split_axis=0, concat_axis=0, tiled=True)
    moved = moved.reshape(n_occ, n_vir, local_j, local_a, local_j, local_a)
    mirror = jnp.transpose(moved, (0, 4, 5, 2, 1, 3)).reshape(batch, local_a, local_j, width)
    return (cycle.astype(jnp.float32) + mirror.astype(jnp.float32)).astype(jnp.bfloat16)


def solution(mesh):
    in_specs = (P(None, "vir", None, None), P(None, "vir", "occ", None), P(), P(), P())
    out_specs = P(None, "vir", "occ", None)
    return jax.shard_map(shards, mesh=mesh, in_specs=in_specs, out_specs=out_specs, check_vma=False)
```

time: 249 us -> 192 us (0.77)
  waiting for transfers between devices: 88.4 us -> 46.3 us
  other arithmetic: 43.5 us -> 20.9 us
  local copies, waits for them, and re-layouts: 58.1 us -> 64.6 us
    all_gather x1, waiting for transfers between devices: 87.7 us -> 46.3 us  [shards(): panels = lax.all_gather(packed, 'vir', axis=1, tiled=True)]
    select_n x1 -> x0, other arithmetic: 24.8 us -> none  [shards(): masked = jnp.where(pmask, piece, jnp.zeros_like(piece))]
    unnamed x4 -> x10, local copies, waits for them, and re-layouts: 19.5 us -> 22.2 us
    reshape x2 -> x4, local copies, waits for them, and re-layouts: 14.8 us -> 15.9 us  [the longest x2 14.8 us: shards(): moved = cycle.reshape(n_occ, local_j, local_a, local_j, n_vir, local_a)]
    dot_general x1 -> x3, matrix products: 12.1 us -> 13.1 us  [the longest x1 7.55 us: shards(): jnp.einsum('iakc,kcn->ian', tsym, panels, preferred_element_type=jnp.floa...]
where the time goes in v1:
time: 192 us; the launch traced here: 191 us
  local copies, waits for them, and re-layouts  64.6 us (34%)
  waiting for transfers between devices  46.3 us (24%)
  blocking collectives  32.8 us (17%)
  other arithmetic  20.9 us (11%)
  between operations  13.5 us (7%)
  matrix products  13.1 us (7%)
    all_gather x1, waiting for transfers between devices, shards(): panels = lax.all_gather(packed, 'vir', axis=1, tiled=True)  46.3 us
    all_to_all x1, blocking collectives, shards(): lax.all_to_all(moved, ('occ', 'vir'), split_axis=0, concat_axis=0, tiled=...  32.8 us
    unnamed x10, local copies, waits for them, and re-layouts  22.2 us
    convert_element_type x2, local copies, waits for them, and re-layouts, shards(): mirror.astype(jnp.float32)  21.3 us
    reshape x2, local copies, waits for them, and re-layouts, shards(): moved = cycle.reshape(n_occ, local_j, local_a, local_j, n_vir, local_a)  14.8 us
    convert_element_type x1, other arithmetic, shards(): mirror.astype(jnp.float32)  7.93 us
    dot_general x1, matrix products, shards(): jnp.einsum('iakc,kcn->ian', tsym, panels, preferred_element_type=jnp.floa...  7.55 us
    select_n x1, other arithmetic, shards(): tsym = jnp.where(tmask, amplitude, jnp.zeros_like(amplitude))  6.19 us
  transfers between devices with their start and end apart: 1, of which 1 were waited for; matrix products, arithmetic and copies ran while one was open for 4% of the time, Pallas kernels for 0%

profile of v1, /device:TPU:1, one launch (start us, length us, event | category | flops | bytes accessed | tf_op | source)
XLA Modules:
  0.0 191.2 jit_solution(1676063055753475837)
XLA Ops:
  6.5 0.0 copy-start
  6.5 0.0 all-gather.2.cloned.1.call-start
  6.5 1.4 dynamic_slice.6
  8.0 0.9 broadcast_xor_fusion
  8.8 0.7 dynamic_slice.7
  9.6 1.4 xor_xor_fusion
  11.0 0.1 copy.20
  11.1 0.8 broadcast_compare_fusion.2
  11.9 0.2 select_reduce_fusion
  12.1 0.1 copy.19
  12.2 0.1 iota_add_fusion.1
  12.2 0.0 copy-done
  12.3 0.0 copy-start.3
  12.3 0.0 copy-start.2
  12.3 2.0 %fusion.32 = bf16[8,40,2,160]{3,1,2,0:T(8,128)(2,1)S(1)} fusion(s32[8,2,160]{2,1,0:T(2,128)S(1)} %iota_add_fusion.1, pred[8,2,640]{2,1,0:T(4,128)(4,1)S(1)} %broadcast_compare_fusion.2, bf16[8,40,2,640]{3,2,1,0:T(2,128)(2,1)S(1)} %copy-done), kind=kOutput, calls=%fused_computation.21 | convolution fusion | flops 134451200 | bytes 1044480 | tf_op jit(solution)/shard_map/kcjb,kjbn->kcjn/dot_general | solution.py:32
  14.3 0.3 copy.22
  14.5 0.9 reshape.178
  15.4 0.0 all-gather.2.cloned.1.call-update
  15.4 0.0 copy-done.3
  15.4 0.7 broadcast_xor_fusion.2
  16.1 0.1 broadcast_xor_fusion.1
  16.2 0.1 copy.18
  16.3 0.1 select_reduce_fusion.1
  16.4 0.1 copy.17
  16.5 0.1 iota_add_fusion
  16.6 0.0 copy-done.2
  16.6 0.1 broadcast_compare_fusion.1
  16.7 0.1 broadcast_compare_fusion
  16.8 6.2 %broadcast_select_fusion = bf16[16,40,8,640]{3,2,1,0:T(8,128)(2,1)} fusion(bf16[16,40,8,640]{3,2,1,0:T(8,128)(2,1)} %param.5, pred[16,8,640]{2,1,0:T(8,128)(4,1)S(1)} %broadcast_compare_fusion), kind=kLoop, calls=%fused_computation.9 | loop fusion | flops 3276800 | bytes 13189120 | tf_op jit(solution)/shard_map/jit(_where)/select_n | solution.py:40
  23.0 46.3 %all-gather.2.cloned.1.call-done = bf16[8,640,320]{2,1,0:T(8,128)(2,1)} async-done(((bf16[8,40,320]{2,1,0:T(8,128)(2,1)}), bf16[8,640,320]{2,1,0:T(8,128)(2,1)}) %all-gather.2.cloned.1.call-update) | async-done | bytes 3276816 | tf_op jit(solution)/shard_map/all_gather | solution.py:36
  69.3 7.5 %fusion.24 = bf16[16,40,320]{2,1,0:T(8,128)(2,1)S(1)} fusion(bf16[8,640,320]{2,1,0:T(8,128)(2,1)} %all-gather.2.cloned.1.call-done, bf16[16,40,8,640]{3,2,1,0:T(8,128)(2,1)} %broadcast_select_fusion), kind=kOutput, calls=%fused_computation.19 | convolution fusion | flops 2097356800 | bytes 10240000 | tf_op jit(solution)/shard_map/iakc,kcn->ian/dot_general | solution.py:41
  76.8 0.2 reshape.179
  77.1 3.6 %fusion.16 = bf16[16,40,2,640]{3,1,2,0:T(8,128)(2,1)S(1)} fusion(s32[16,2,160]{2,1,0:T(2,128)S(1)} %iota_add_fusion, pred[16,2,640]{2,1,0:T(4,128)(4,1)S(1)} %broadcast_compare_fusion.1, bf16[16,40,2,160]{3,2,1,0:T(2,128)(2,1)S(1)} %reshape.179), kind=kOutput, calls=%fused_computation.17 | convolution fusion | flops 269516800 | bytes 2088960 | tf_op jit(solution)/shard_map/iajn,ijbn->iajb/dot_general | solution.py:45
  80.7 8.6 %reshape.180 = bf16[8,2,40,2,16,40]{5,4,2,3,1,0:T(8,128)(2,1)} reshape(bf16[16,40,2,640]{3,1,2,0:T(8,128)(2,1)S(1)} %fusion.16) | data formatting | bytes 3276800 | tf_op jit(solution)/shard_map/reshape | solution.py:49
  89.2 6.2 %copy.25 = bf16[8,2,40,2,16,40]{5,2,3,1,4,0:T(8,128)(2,1)} copy(bf16[8,2,40,2,16,40]{5,4,2,3,1,0:T(8,128)(2,1)} %reshape.180) | data formatting | bytes 3276800 | tf_op jit(solution)/shard_map/reshape | solution.py:49
  95.4 10.8 %reshape.186 = bf16[128,2,3200]{2,1,0:T(2,128)(2,1)} reshape(bf16[256,2,40,40]{3,2,1,0:T(8,128)(2,1)} %bitcast.34) | data formatting | bytes 3276800
  106.2 32.8 %all_to_all.5 = bf16[128,2,3200]{2,1,0:T(2,128)(2,1)} all-to-all(bf16[128,2,3200]{2,1,0:T(2,128)(2,1)} %reshape.186), channel_id=1, replica_groups=mesh['occ'=8,'vir'=16] {'occ','vir'}, dimensions={0} | all-to-all | bytes 3276800 | tf_op jit(solution)/shard_map/all_to_all | solution.py:51
  139.0 11.4 %reshape.187 = bf16[256,2,40,40]{3,2,1,0:T(8,128)(2,1)} reshape(bf16[128,2,3200]{2,1,0:T(2,128)(2,1)} %all_to_all.5) | data formatting | bytes 3276800
  150.4 7.9 %convert_bitcast_fusion = f32[8,2,40,2,16,40]{2,5,1,3,4,0:T(8,128)} fusion(bf16[8,16,2,40,2,40]{5,3,4,2,1,0:T(8,128)(2,1)} %bitcast.35), kind=kLoop, calls=%fused_computation.3 | loop fusion | flops 819200 | bytes 4915200 | tf_op jit(solution)/shard_map/convert_element_type | solution.py:54
  158.4 11.7 %copy.26 = f32[8,2,40,2,16,40]{5,4,2,3,1,0:T(8,128)} copy(f32[8,2,40,2,16,40]{2,5,1,3,4,0:T(8,128)} %convert_bitcast_fusion) | data formatting | bytes 6553600 | tf_op jit(solution)/shard_map/convert_element_type | solution.py:54
  170.1 0.0 copy-start.1
  170.1 9.5 %reshape.182 = f32[16,40,2,640]{3,1,2,0:T(8,128)} reshape(f32[8,2,40,2,16,40]{5,4,2,3,1,0:T(8,128)} %copy.26) | data formatting | bytes 6553600 | tf_op jit(solution)/shard_map/convert_element_type | solution.py:54
  179.6 2.3 %add_convert_fusion = bf16[16,40,2,640]{3,1,2,0:T(8,128)(2,1)S(1)} fusion(f32[16,40,2,640]{3,1,2,0:T(8,128)} %reshape.182, bf16[16,40,2,640]{3,1,2,0:T(8,128)(2,1)S(1)} %fusion.16), kind=kLoop, calls=%fused_computation.13 | loop fusion | flops 2457600 | bytes 6553600 | tf_op jit(solution)/shard_map/convert_element_type | solution.py:54
  181.9 2.4 %copy.27 = bf16[16,40,2,640]{3,2,1,0:T(2,128)(2,1)} copy(bf16[16,40,2,640]{3,1,2,0:T(8,128)(2,1)S(1)} %add_convert_fusion) | data formatting | bytes 3276800 | tf_op jit(solution)/shard_map/convert_element_type | solution.py:54
  184.3 0.0 copy-done.1
  (1 shorter events, 0.0 us)
Async XLA Ops:
  6.5 5.7 %copy-start = (bf16[8,40,2,640]{3,2,1,0:T(2,128)(2,1)S(1)}, bf16[8,40,2,640]{3,2,1,0:T(2,128)(2,1)}, u32[]{:S(2)}) copy-start(bf16[8,40,2,640]{3,2,1,0:T(2,128)(2,1)} %param.6) | copy-start | bytes 2457604
  6.5 62.8 %all-gather.2.cloned.1.call-start = ((), (), s32[]{:S(2)}) async-start(), calls=%async_computation.1 | async-start | bytes 4177920 | tf_op jit(solution)/shard_map/all_gather | solution.py:36
  12.3 3.2 %copy-start.3 = (s32[16]{0:T(128)S(1)}, s32[16]{0:T(128)}, u32[]{:S(2)}) copy-start(s32[16]{0:T(128)} %param.7) | copy-start | bytes 196
  12.3 4.3 %copy-start.2 = (s32[640]{0:T(1024)S(1)}, s32[640]{0:T(1024)}, u32[]{:S(2)}) copy-start(s32[640]{0:T(1024)} %param.9) | copy-start | bytes 7684
  170.1 14.2 %copy-start.1 = (bf16[8,40,2,640]{3,2,1,0:T(2,128)(2,1)S(1)}, bf16[8,40,2,640]{3,2,1,0:T(2,128)(2,1)}, u32[]{:S(2)}) copy-start(bf16[8,40,2,640]{3,2,1,0:T(2,128)(2,1)} %param.6) | copy-start | bytes 2457604
Sparse Core Ops, SparseCore 0:
  15.5 53.6 all-gather.1

commit v2 on v1

--- a/solution.py
+++ b/solution.py
@@ -1,9 +1,189 @@
+import functools
 import jax
 import jax.numpy as jnp
 from jax import lax
+from jax.experimental import pallas as pl
+from jax.experimental.pallas import tpu as pltpu
 from jax.sharding import PartitionSpec as P
 
 WIN = 160
+MESH = pl.DeviceIdType.MESH
+CUT = 48
+
+
+def gather_product(amp_ref, pack_ref, occ_ref, kocc_ref, lab_ref, virs_ref, out_ref,
+                   amp, panels, tk, wk, acc, amp_sem, own_sem, send_sem, recv_sem):
+    me = lax.axis_index("vir")
+    z, x = me // 4, lax.rem(me, 4)
+    batch, la, nk, nv = amp.shape
+    pairs = batch // 2
+
+    def amp_copy(i):
+        return pltpu.make_async_copy(amp_ref.at[pl.ds(2 * i, 2)], amp.at[pl.ds(2 * i, 2)], amp_sem.at[i])
+
+    for i in range(pairs):
+        amp_copy(i).start()
+
+    def at(h, p, q):
+        p, q = lax.rem(p + 8, 4), lax.rem(q + 8, 4)
+        return q * 4 + p if h == 0 else p * 4 + q
+
+    here = [(x, z), (z, x)]
+    barrier = pltpu.get_barrier_semaphore()
+    for dp, dq in ((1, 0), (-1, 0), (0, 1), (0, -1)):
+        pl.semaphore_signal(barrier, inc=1, device_id={"vir": at(0, x + dp, z + dq)}, device_id_type=MESH)
+    own = [pltpu.make_async_copy(pack_ref.at[h], panels.at[h, me], own_sem.at[h]) for h in range(2)]
+    for c in own:
+        c.start()
+    pl.semaphore_wait(barrier, 4)
+
+    copies = []
+
+    def send(h, block, rows, step, slot):
+        p, q = here[h]
+        v = at(h, p + block[0], q + block[1])
+        ref = panels.at[h, v, pl.ds(rows[0], rows[1] - rows[0])]
+        if block == (0, 0):
+            src = pack_ref.at[h, pl.ds(rows[0], rows[1] - rows[0])]
+        else:
+            src = ref
+        c = pltpu.make_async_remote_copy(
+            src_ref=src, dst_ref=ref, send_sem=send_sem.at[h, slot], recv_sem=recv_sem.at[h, slot],
+            device_id={"vir": at(h, p + step[0], q + step[1])}, device_id_type=MESH)
+        c.start()
+        copies.append(c)
+
+    def arrived(h, block, rows, slot):
+        p, q = here[h]
+        v = at(h, p + block[0], q + block[1])
+        ref = panels.at[h, v, pl.ds(rows[0], rows[1] - rows[0])]
+        pltpu.make_async_remote_copy(
+            src_ref=ref, dst_ref=ref, send_sem=send_sem.at[h, slot], recv_sem=recv_sem.at[h, slot],
+            device_id={"vir": me}, device_id_type=MESH).wait_recv()
+
+    full, low, high = (0, 2 * la), (0, CUT), (CUT, 2 * la)
+
+    def second(h, d):
+        send(h, (d, 0), full, (0, 1), 4 + 4 * d)
+        send(h, (d, 0), full, (0, -1), 5 + 4 * d)
+
+    rows = la * nk
+    r = lax.broadcasted_iota(jnp.int32, (rows, rows), 0)
+    c = lax.broadcasted_iota(jnp.int32, (rows, rows), 1)
+    perm = (c == lax.rem(r, la) * nk + r // la).astype(jnp.float32).astype(jnp.bfloat16)
+    mylab = virs_ref[me * la]
+
+    def prepare(i):
+        amp_copy(i).wait()
+        parts = []
+        for s in range(2):
+            flat = amp[2 * i + s].reshape(rows, nv)
+            moved = jnp.dot(perm, flat, preferred_element_type=jnp.float32)
+            left = occ_ref[2 * i + s] ^ mylab
+            parts.append([
+                jnp.where(lab_ref[...] == (left ^ kocc_ref[k]), moved[k * la:(k + 1) * la], 0.0)
+                for k in range(nk)])
+        for k in range(nk):
+            tk[k, pl.ds(2 * la * i, 2 * la), :] = jnp.concatenate(
+                [parts[0][k], parts[1][k]], axis=0).astype(jnp.bfloat16)
+
+    for h in range(2):
+        send(h, (0, 0), full, (1, 0), 0)
+        send(h, (0, 0), full, (-1, 0), 1)
+        second(h, 0)
+    prepare(0)
+    prepare(1)
+    for h in range(2):
+        arrived(h, (-1, 0), full, 0)
+        send(h, (-1, 0), low, (1, 0), 2)
+        second(h, 3)
+        arrived(h, (1, 0), full, 1)
+        send(h, (1, 0), high, (-1, 0), 3)
+        second(h, 1)
+
+    def relay(h, d):
+        b = d if d < 2 else d - 4
+        arrived(h, (b, -1), full, 4 + 4 * d)
+        send(h, (b, -1), low, (0, 1), 6 + 4 * d)
+        arrived(h, (b, 1), full, 5 + 4 * d)
+        send(h, (b, 1), high, (0, -1), 7 + 4 * d)
+
+    prepare(2)
+    for h in range(2):
+        relay(h, 0)
+    prepare(3)
+    for h in range(2):
+        arrived(h, (-2, 0), low, 2)
+        arrived(h, (-2, 0), high, 3)
+        second(h, 2)
+    prepare(4)
+    for h in range(2):
+        relay(h, 3)
+    prepare(5)
+    for h in range(2):
+        relay(h, 1)
+    prepare(6)
+    prepare(7)
+    for h in range(2):
+        relay(h, 2)
+    for h in range(2):
+        for d in range(4):
+            b = d if d < 2 else d - 4
+            arrived(h, (b, 2), low, 6 + 4 * d)
+            arrived(h, (b, 2), high, 7 + 4 * d)
+    for c in own:
+        c.wait()
+    for h in range(2):
+        for v in range(0, 16, 2):
+            one = panels[h, v].astype(jnp.float32)
+            two = panels[h, v + 1].astype(jnp.float32)
+            for kp in range(2):
+                wk[kp, pl.ds(v * la, 2 * la), :] = jnp.concatenate(
+                    [one[kp * la:(kp + 1) * la], two[kp * la:(kp + 1) * la]], axis=0).astype(jnp.bfloat16)
+        for kp in range(2):
+            k = 4 * h + 2 * kp
+            a = jnp.dot(tk[k], wk[kp, :, 0:384], preferred_element_type=jnp.float32)
+            b = jnp.dot(tk[k + 1], wk[kp, :, 256:640], preferred_element_type=jnp.float32)
+            if k == 0:
+                acc[0] = a
+                acc[1] = b
+            else:
+                acc[0] += a
+                acc[1] += b
+    out_ref[...] = (acc[0][:, 0:320] + acc[1][:, 64:384]).astype(jnp.bfloat16)
+    for c in copies:
+        c.wait_send()
+
+
+def cycle_windows(amplitude, pack, occ_irrep, kocc_irrep, vir_irrep):
+    batch, la, nk, nv = amplitude.shape
+    return pl.pallas_call(
+        gather_product,
+        out_shape=jax.ShapeDtypeStruct((batch * la, 320), jnp.bfloat16),
+        in_specs=[
+            pl.BlockSpec(memory_space=pl.ANY),
+            pl.BlockSpec(memory_space=pltpu.VMEM),
+            pl.BlockSpec(memory_space=pltpu.SMEM),
+            pl.BlockSpec(memory_space=pltpu.SMEM),
+            pl.BlockSpec(memory_space=pltpu.VMEM),
+            pl.BlockSpec(memory_space=pltpu.SMEM),
+        ],
+        out_specs=pl.BlockSpec(memory_space=pltpu.VMEM),
+        scratch_shapes=[
+            pltpu.VMEM((batch, la, nk, nv), jnp.bfloat16),
+            pltpu.VMEM((2, 16, 2 * la, 640), jnp.bfloat16),
+            pltpu.VMEM((nk, batch * la, nv), jnp.bfloat16),
+            pltpu.VMEM((2, nv, 640), jnp.bfloat16),
+            pltpu.VMEM((2, batch * la, 384), jnp.float32),
+            pltpu.SemaphoreType.DMA((batch // 2,)),
+            pltpu.SemaphoreType.DMA((2,)),
+            pltpu.SemaphoreType.DMA((2, 20)),
+            pltpu.SemaphoreType.DMA((2, 20)),
+        ],
+        compiler_params=pltpu.CompilerParams(
+            collective_id=0, has_side_effects=True, vmem_limit_bytes=48 * 1024 * 1024),
+        name="gather_product",
+    )(amplitude, pack, occ_irrep, kocc_irrep, vir_irrep.reshape(1, -1), vir_irrep)
 
 
 def shards(amplitude, integral, occ_irrep, kocc_irrep, vir_irrep):
@@ -32,14 +212,10 @@
     packed = jnp.einsum(
         "kcjb,kjbn->kcjn", integral, select(wlab), preferred_element_type=jnp.float32
     ).astype(jnp.bfloat16)
-    packed = packed.reshape(packed.shape[0], local_a, local_j * WIN)
-    panels = lax.all_gather(packed, "vir", axis=1, tiled=True)
+    packed = jnp.transpose(packed.reshape(2, 2, 2, local_a, local_j * WIN), (0, 1, 3, 2, 4)).reshape(2, 2 * local_a, 640)
+    cyc = cycle_windows(amplitude, packed, occ_irrep, kocc_irrep, vir_irrep)
     left = occ_irrep ^ own
-    right = kocc_irrep[:, None] ^ vir_irrep[None, :]
-    tmask = left[:, None, None, None] == right[None, None, :, :]
-    tsym = jnp.where(tmask, amplitude, jnp.zeros_like(amplitude))
-    cyc = jnp.einsum("iakc,kcn->ian", tsym, panels, preferred_element_type=jnp.float32).astype(jnp.bfloat16)
-    batch = cyc.shape[0]
+    batch = amplitude.shape[0]
     cyc = cyc.reshape(batch, local_a, local_j, WIN)
     clab = left[:, None] ^ j_labels[None, :]
     cycle = jnp.einsum(

time: 192 us -> 152 us (0.79)
  waiting for transfers between devices: 46.3 us -> 0 us
  Pallas kernels: 0 us -> 30.3 us
  between operations: 13.5 us -> 0.16 us
  matrix products: 13.1 us -> 5.53 us
  other arithmetic: 20.9 us -> 15.9 us
    all_gather x1 -> x0, waiting for transfers between devices: 46.3 us -> none  [shards(): panels = lax.all_gather(packed, 'vir', axis=1, tiled=True)]
    pallas_call x0 -> x1, Pallas kernels: none -> 30.3 us  [cycle_windows(): pl.pallas_call(gather_product, out_shape=jax.ShapeDtypeStruct((batch * la...]
    dot_general x1 -> x0, matrix products: 7.55 us -> none  [shards(): jnp.einsum('iakc,kcn->ian', tsym, panels, preferred_element_type=jnp.floa...]
    select_n x1 -> x0, other arithmetic: 6.19 us -> none  [shards(): tsym = jnp.where(tmask, amplitude, jnp.zeros_like(amplitude))]
  transfers between devices with their start and end apart: 1 -> 0, of which waited for: 1 -> 0; matrix products, arithmetic and copies ran while one was open for 4% -> 0% of each run, Pallas kernels for 0% -> 0%
where the time goes in v2:
time: 152 us; the launch traced here: 151 us
  local copies, waits for them, and re-layouts  64.7 us (43%)
  blocking collectives  34.6 us (23%)
  Pallas kernels  30.3 us (20%)
  other arithmetic  15.9 us (10%)
  matrix products  5.53 us (4%)
    all_to_all x1, blocking collectives, shards(): lax.all_to_all(moved, ('occ', 'vir'), split_axis=0, concat_axis=0, tiled=...  34.6 us
    pallas_call x1, Pallas kernels, cycle_windows(): pl.pallas_call(gather_product, out_shape=jax.ShapeDtypeStruct((batch * la...  30.3 us
    unnamed x10, local copies, waits for them, and re-layouts  22.2 us
    convert_element_type x2, local copies, waits for them, and re-layouts, shards(): mirror.astype(jnp.float32)  21.2 us
    reshape x2, local copies, waits for them, and re-layouts, shards(): moved = cycle.reshape(n_occ, local_j, local_a, local_j, n_vir, local_a)  14.8 us
    convert_element_type x1, other arithmetic, shards(): mirror.astype(jnp.float32)  7.93 us
    dot_general x1, matrix products, shards(): jnp.einsum('iajn,ijbn->iajb', cyc, select(clab), preferred_element_type=j...  3.56 us

profile of v2, /device:TPU:1, one launch (start us, length us, event | category | flops | bytes accessed | tf_op | source)
XLA Modules:
  0.0 151.2 jit_solution(17838310227576432203)
XLA Ops:
  0.0 0.0 copy-start
  0.0 0.9 convert_reduce_fusion
  0.9 0.7 broadcast_in_dim.36.lab_ref
  1.6 1.3 dynamic_slice.6
  2.8 0.7 dynamic_slice.7
  3.6 1.3 broadcast_xor_fusion.1
  4.9 1.4 xor_xor_fusion
  6.2 0.1 broadcast_xor_fusion
  6.3 0.1 copy.19
  6.4 0.2 select_reduce_fusion
  6.6 0.1 select_reduce_fusion.1
  6.7 0.1 copy.17
  6.8 0.1 copy.18
  6.9 0.1 copy.16
  6.9 0.1 iota_add_fusion.1
  7.0 0.8 broadcast_compare_fusion.1
  7.8 0.1 iota_add_fusion
  7.9 0.8 broadcast_compare_fusion
  8.7 0.0 copy-done
  8.7 0.0 copy-start.1
  8.7 0.0 copy-start.2
  8.7 0.0 copy-start.3
  8.8 2.0 %fusion.19 = bf16[8,40,2,160]{3,1,2,0:T(8,128)(2,1)S(1)} fusion(s32[8,2,160]{2,1,0:T(2,128)S(1)} %iota_add_fusion.1, pred[8,2,640]{2,1,0:T(4,128)(4,1)S(1)} %broadcast_compare_fusion.1, bf16[8,40,2,640]{3,2,1,0:T(2,128)(2,1)S(1)} %copy-done), kind=kOutput, calls=%fused_computation.15 | convolution fusion | flops 134451200 | bytes 1044480 | tf_op jit(solution)/shard_map/kcjb,kjbn->kcjn/dot_general | solution.py:212
  10.7 0.3 copy.21
  11.0 0.2 reshape.152
  11.2 0.2 copy.22
  11.4 0.2 reshape.153.pack_ref
  11.6 0.0 copy-done.1
  11.6 0.0 copy-done.2
  11.6 0.0 copy-done.3
  11.6 30.3 %gather_product.1 = bf16[640,320]{1,0:T(8,128)(2,1)S(1)} custom-call(bf16[16,40,8,640]{3,2,1,0:T(8,128)(2,1)} %amp_ref.1, bf16[2,80,640]{2,1,0:T(8,128)(2,1)S(1)} %reshape.153.pack_ref, s32[16]{0:T(128)S(1)} %copy-done.3, s32[8]{0:T(128)S(1)} %copy-done.2, s32[1,640]{1,0:T(1,128)S(1)} %broadcast_in_dim.36.lab_ref, s32[640]{0:T(1024)S(1)} %copy-done.1), custom_call_target="tpu_custom_call" | custom-call | tf_op jit(solution)/shard_map/gather_product/pallas_call | solution.py:160
  41.9 0.2 reshape.154
  42.1 3.6 %fusion.13 = bf16[16,40,2,640]{3,1,2,0:T(8,128)(2,1)S(1)} fusion(s32[16,2,160]{2,1,0:T(2,128)S(1)} %iota_add_fusion, pred[16,2,640]{2,1,0:T(4,128)(4,1)S(1)} %broadcast_compare_fusion, bf16[16,40,2,160]{3,2,1,0:T(2,128)(2,1)S(1)} %reshape.154), kind=kOutput, calls=%fused_computation.13 | convolution fusion | flops 269516800 | bytes 2088960 | tf_op jit(solution)/shard_map/iajn,ijbn->iajb/dot_general | solution.py:221
  45.7 8.6 %reshape.155 = bf16[8,2,40,2,16,40]{5,4,2,3,1,0:T(8,128)(2,1)} reshape(bf16[16,40,2,640]{3,1,2,0:T(8,128)(2,1)S(1)} %fusion.13) | data formatting | bytes 3276800 | tf_op jit(solution)/shard_map/reshape | solution.py:225
  54.3 6.2 %copy.24 = bf16[8,2,40,2,16,40]{5,2,3,1,4,0:T(8,128)(2,1)} copy(bf16[8,2,40,2,16,40]{5,4,2,3,1,0:T(8,128)(2,1)} %reshape.155) | data formatting | bytes 3276800 | tf_op jit(solution)/shard_map/reshape | solution.py:225
  60.5 10.8 %reshape.159 = bf16[128,2,3200]{2,1,0:T(2,128)(2,1)} reshape(bf16[256,2,40,40]{3,2,1,0:T(8,128)(2,1)} %bitcast.23) | data formatting | bytes 3276800
  71.3 34.6 %all_to_all.5 = bf16[128,2,3200]{2,1,0:T(2,128)(2,1)} all-to-all(bf16[128,2,3200]{2,1,0:T(2,128)(2,1)} %reshape.159), channel_id=1, replica_groups=mesh['occ'=8,'vir'=16] {'occ','vir'}, dimensions={0} | all-to-all | bytes 3276800 | tf_op jit(solution)/shard_map/all_to_all | solution.py:227
  105.9 11.4 %reshape.160 = bf16[256,2,40,40]{3,2,1,0:T(8,128)(2,1)} reshape(bf16[128,2,3200]{2,1,0:T(2,128)(2,1)} %all_to_all.5) | data formatting | bytes 3276800
  117.3 7.9 %convert_bitcast_fusion = f32[8,2,40,2,16,40]{2,5,1,3,4,0:T(8,128)} fusion(bf16[8,16,2,40,2,40]{5,3,4,2,1,0:T(8,128)(2,1)} %bitcast.24), kind=kLoop, calls=%fused_computation.3 | loop fusion | flops 819200 | bytes 4915200 | tf_op jit(solution)/shard_map/convert_element_type | solution.py:230
  125.3 11.7 %copy.25 = f32[8,2,40,2,16,40]{5,4,2,3,1,0:T(8,128)} copy(f32[8,2,40,2,16,40]{2,5,1,3,4,0:T(8,128)} %convert_bitcast_fusion) | data formatting | bytes 6553600 | tf_op jit(solution)/shard_map/convert_element_type | solution.py:230
  137.0 9.5 %reshape.157 = f32[16,40,2,640]{3,1,2,0:T(8,128)} reshape(f32[8,2,40,2,16,40]{5,4,2,3,1,0:T(8,128)} %copy.25) | data formatting | bytes 6553600 | tf_op jit(solution)/shard_map/convert_element_type | solution.py:230
  146.5 2.3 %add_convert_fusion = bf16[16,40,2,640]{3,1,2,0:T(8,128)(2,1)S(1)} fusion(f32[16,40,2,640]{3,1,2,0:T(8,128)} %reshape.157, bf16[16,40,2,640]{3,1,2,0:T(8,128)(2,1)S(1)} %fusion.13), kind=kLoop, calls=%fused_computation.9 | loop fusion | flops 2457600 | bytes 6553600 | tf_op jit(solution)/shard_map/convert_element_type | solution.py:230
  148.8 2.4 %copy.26 = bf16[16,40,2,640]{3,2,1,0:T(2,128)(2,1)} copy(bf16[16,40,2,640]{3,1,2,0:T(8,128)(2,1)S(1)} %add_convert_fusion) | data formatting | bytes 3276800 | tf_op jit(solution)/shard_map/convert_element_type | solution.py:230
  (1 shorter events, 0.0 us)
Async XLA Ops:
  0.0 8.7 %copy-start = (bf16[8,40,2,640]{3,2,1,0:T(2,128)(2,1)S(1)}, bf16[8,40,2,640]{3,2,1,0:T(2,128)(2,1)}, u32[]{:S(2)}) copy-start(bf16[8,40,2,640]{3,2,1,0:T(2,128)(2,1)} %param.6) | copy-start | bytes 2457604
  8.7 2.9 %copy-start.1 = (s32[640]{0:T(1024)S(1)}, s32[640]{0:T(1024)}, u32[]{:S(2)}) copy-start(s32[640]{0:T(1024)} %virs_ref.1) | copy-start | bytes 7684
  8.7 2.9 %copy-start.2 = (s32[8]{0:T(128)S(1)}, s32[8]{0:T(128)}, u32[]{:S(2)}) copy-start(s32[8]{0:T(128)} %kocc_ref.1) | copy-start | bytes 100
  8.7 2.9 %copy-start.3 = (s32[16]{0:T(128)S(1)}, s32[16]{0:T(128)}, u32[]{:S(2)}) copy-start(s32[16]{0:T(128)} %occ_ref.1) | copy-start | bytes 196

commit v3 on v2

--- a/solution.py
+++ b/solution.py
@@ -7,13 +7,17 @@
 from jax.sharding import PartitionSpec as P
 
 WIN = 160
+FEW = 6
 MESH = pl.DeviceIdType.MESH
 CUT = 48
 
 
-def gather_product(amp_ref, pack_ref, occ_ref, kocc_ref, lab_ref, virs_ref, out_ref,
-                   amp, panels, tk, wk, acc, amp_sem, own_sem, send_sem, recv_sem):
+def cycle_kernel(groups, amp_ref, pack_ref, occ_ref, kocc_ref, lab_ref, virs_ref,
+                 order, place, begin, block_of, group_of, member_of, out_ref,
+                 amp, panels, tk, wk, acc, cw, comb, far, near, nearf, turned, pack_out, pack_in,
+                 amp_sem, own_sem, send_sem, recv_sem, far_send, far_recv, occ_send, occ_recv):
     me = lax.axis_index("vir")
+    mine = lax.axis_index("occ")
     z, x = me // 4, lax.rem(me, 4)
     batch, la, nk, nv = amp.shape
     pairs = batch // 2
@@ -30,12 +34,15 @@
 
     here = [(x, z), (z, x)]
     barrier = pltpu.get_barrier_semaphore()
-    for dp, dq in ((1, 0), (-1, 0), (0, 1), (0, -1)):
-        pl.semaphore_signal(barrier, inc=1, device_id={"vir": at(0, x + dp, z + dq)}, device_id_type=MESH)
+    for off in range(1, 16):
+        pl.semaphore_signal(barrier, inc=1, device_id={"vir": at(0, x + off % 4, z + off // 4)}, device_id_type=MESH)
+    for off in range(1, 8):
+        pl.semaphore_signal(barrier, inc=1, device_id={"occ": lax.rem(mine + off, 8)}, device_id_type=MESH)
     own = [pltpu.make_async_copy(pack_ref.at[h], panels.at[h, me], own_sem.at[h]) for h in range(2)]
     for c in own:
         c.start()
-    pl.semaphore_wait(barrier, 4)
+
+    pl.semaphore_wait(barrier, 22)
 
     copies = []
 
@@ -73,13 +80,16 @@
     perm = (c == lax.rem(r, la) * nk + r // la).astype(jnp.float32).astype(jnp.bfloat16)
     mylab = virs_ref[me * la]
 
+    for i in range(pairs):
+        amp_copy(i).wait()
+
     def prepare(i):
-        amp_copy(i).wait()
         parts = []
         for s in range(2):
-            flat = amp[2 * i + s].reshape(rows, nv)
+            orb = order[2 * i + s]
+            flat = amp[orb].reshape(rows, nv)
             moved = jnp.dot(perm, flat, preferred_element_type=jnp.float32)
-            left = occ_ref[2 * i + s] ^ mylab
+            left = occ_ref[orb] ^ mylab
             parts.append([
                 jnp.where(lab_ref[...] == (left ^ kocc_ref[k]), moved[k * la:(k + 1) * la], 0.0)
                 for k in range(nk)])
@@ -150,16 +160,126 @@
             else:
                 acc[0] += a
                 acc[1] += b
-    out_ref[...] = (acc[0][:, 0:320] + acc[1][:, 64:384]).astype(jnp.bfloat16)
+    whole = acc[0] + pltpu.roll(acc[1], 320, 1)
+    wide = lax.broadcasted_iota(jnp.int32, whole.shape, 1)
+    flatw = jnp.where(wide < 2 * WIN, whole, 0.0).astype(jnp.bfloat16).astype(jnp.float32)
+    cw[...] = flatw.reshape(batch, la, 384)
+    jocc = [occ_ref[2 * mine + j] for j in range(2)]
+
+    spot = lax.broadcasted_iota(jnp.int32, (batch * la, 128), 1)
+    for j in range(2):
+        for r in range(4):
+            start = WIN * j + la * r
+            tile = start // 128 * 128
+            width = 128 if start + la <= tile + 128 else 256
+            total = None
+            for g in range(3):
+                piece = flatw[g * la:, tile:tile + width]
+                shift = (la * g - (start - tile)) % width
+                if shift:
+                    piece = pltpu.roll(piece, shift, 1)
+                piece = piece[:, :128]
+                if g:
+                    piece = jnp.concatenate([piece, jnp.zeros((g * la, 128), jnp.float32)], axis=0)
+                total = piece if g == 0 else jnp.where(spot >= g * la, piece, total)
+            comb[4 * j + r] = total.reshape(batch, la, 128)
+
+    def message(r, v):
+        lab = virs_ref[v * la]
+        parts = []
+        for j in range(2):
+            base = begin[jocc[j] ^ lab ^ mylab]
+            for q in range(groups):
+                parts.append(comb[4 * j + r, base + 3 * q])
+        return jnp.concatenate(parts, axis=0).astype(jnp.bfloat16)
+
+    def far_copy(off, v, source):
+        return pltpu.make_async_remote_copy(
+            src_ref=far.at[v], dst_ref=near.at[source], send_sem=far_send.at[off], recv_sem=far_recv.at[off],
+            device_id={"vir": v}, device_id_type=MESH)
+
+    offs = [10, 9, 11, 6, 14, 2, 8, 5, 7, 13, 15, 1, 3, 4, 12]
+    for off in offs:
+        v = at(0, x + off % 4, z + off // 4)
+        far[v] = message(lax.rem(x + off % 4, 4), v)
+        far_copy(off, v, me).start()
+    near[me] = message(x, me)
+    nearf[me] = near[me].astype(jnp.float32).reshape(2 * groups, la, 128)
+    for off in reversed(offs):
+        source = at(0, x - off % 4, z - off // 4)
+        pltpu.make_async_remote_copy(
+            src_ref=near.at[source], dst_ref=near.at[source], send_sem=far_send.at[off], recv_sem=far_recv.at[off],
+            device_id={"vir": source}, device_id_type=MESH).wait_recv()
+        nearf[source] = near[source].astype(jnp.float32).reshape(2 * groups, la, 128)
+
+    def windows(o):
+        both = []
+        for j in range(2):
+            wins = []
+            for s in range(2):
+                orb = 2 * o + s
+                lab = occ_ref[orb]
+                want = lab ^ mylab ^ jocc[j]
+                row = groups * j + group_of[orb]
+                stack = [nearf[block_of[4 * want + d], row] for d in range(4)]
+                stack = jnp.concatenate(stack + [jnp.zeros((96, 128), jnp.float32)], axis=0).T
+                for m in range(3):
+                    turned[2 * j + s, m] = stack[m * la:(m + 1) * la]
+                win = turned[2 * j + s, member_of[orb]]
+                wins.append(jnp.concatenate([win, jnp.zeros((la, 128), jnp.float32)], axis=1))
+            both.append(wins[0] + pltpu.roll(wins[1], WIN, 1))
+        return jnp.concatenate(both, axis=0).astype(jnp.bfloat16)
+
+    def occ_copy(off, o, source):
+        return pltpu.make_async_remote_copy(
+            src_ref=pack_out.at[o], dst_ref=pack_in.at[source], send_sem=occ_send.at[off], recv_sem=occ_recv.at[off],
+            device_id={"occ": o}, device_id_type=MESH)
+
+    order_occ = [4, 5, 3, 2, 6, 7, 1]
+    for off in order_occ:
+        o = lax.rem(mine + off, 8)
+        pack_out[o] = windows(o)
+        occ_copy(off, o, mine).start()
+    pack_in[mine] = windows(mine)
+
+    tile_no = lax.broadcasted_iota(jnp.int32, (la, 640), 1) // WIN
+    even = lax.rem(tile_no, 2) == 0
+
+    def finish(o):
+        back = pack_in[o].astype(jnp.float32)
+        for j2 in range(2):
+            orb = 2 * o + j2
+            own_rows = cw[place[orb]]
+            both = own_rows + back[j2 * la:(j2 + 1) * la]
+            both = jnp.concatenate([both, jnp.zeros((la, 256), jnp.float32)], axis=1)
+            both = both + pltpu.roll(both, 2 * WIN, 1)
+            turn = pltpu.roll(both, WIN, 1)
+            for j in range(2):
+                want = occ_ref[orb] ^ mylab ^ jocc[j]
+                row = jnp.where(even, both, turn) if j == 0 else jnp.where(even, turn, both)
+                out_ref[orb, j] = jnp.where(lab_ref[...] == want, row, 0.0).astype(jnp.bfloat16)
+
+    finish(mine)
+    for off in reversed(order_occ):
+        source = lax.rem(mine + 8 - off, 8)
+        pltpu.make_async_remote_copy(
+            src_ref=pack_in.at[source], dst_ref=pack_in.at[source], send_sem=occ_send.at[off],
+            recv_sem=occ_recv.at[off], device_id={"occ": source}, device_id_type=MESH).wait_recv()
+        finish(source)
     for c in copies:
         c.wait_send()
-
-
-def cycle_windows(amplitude, pack, occ_irrep, kocc_irrep, vir_irrep):
+    for off in offs:
+        far_copy(off, at(0, x + off % 4, z + off // 4), me).wait_send()
+    for off in order_occ:
+        occ_copy(off, lax.rem(mine + off, 8), mine).wait_send()
+
+
+def residual_rows(groups, collective, amplitude, pack, occ_irrep, kocc_irrep, vir_row, vir_irrep, *tables):
     batch, la, nk, nv = amplitude.shape
+    rows = 2 * groups * la
     return pl.pallas_call(
-        gather_product,
-        out_shape=jax.ShapeDtypeStruct((batch * la, 320), jnp.bfloat16),
+        functools.partial(cycle_kernel, groups),
+        out_shape=jax.ShapeDtypeStruct((batch, 2, la, nv), jnp.bfloat16),
         in_specs=[
             pl.BlockSpec(memory_space=pl.ANY),
             pl.BlockSpec(memory_space=pltpu.VMEM),
@@ -167,7 +287,7 @@
             pl.BlockSpec(memory_space=pltpu.SMEM),
             pl.BlockSpec(memory_space=pltpu.VMEM),
             pl.BlockSpec(memory_space=pltpu.SMEM),
-        ],
+        ] + [pl.BlockSpec(memory_space=pltpu.SMEM)] * 6,
         out_specs=pl.BlockSpec(memory_space=pltpu.VMEM),
         scratch_shapes=[
             pltpu.VMEM((batch, la, nk, nv), jnp.bfloat16),
@@ -175,59 +295,110 @@
             pltpu.VMEM((nk, batch * la, nv), jnp.bfloat16),
             pltpu.VMEM((2, nv, 640), jnp.bfloat16),
             pltpu.VMEM((2, batch * la, 384), jnp.float32),
+            pltpu.VMEM((batch, la, 384), jnp.float32),
+            pltpu.VMEM((8, batch, la, 128), jnp.float32),
+            pltpu.VMEM((16, rows, 128), jnp.bfloat16),
+            pltpu.VMEM((16, rows, 128), jnp.bfloat16),
+            pltpu.VMEM((16, 2 * groups, la, 128), jnp.float32),
+            pltpu.VMEM((4, 3, la, 256), jnp.float32),
+            pltpu.VMEM((8, 2 * la, 384), jnp.bfloat16),
+            pltpu.VMEM((8, 2 * la, 384), jnp.bfloat16),
             pltpu.SemaphoreType.DMA((batch // 2,)),
             pltpu.SemaphoreType.DMA((2,)),
             pltpu.SemaphoreType.DMA((2, 20)),
             pltpu.SemaphoreType.DMA((2, 20)),
+            pltpu.SemaphoreType.DMA((16,)),
+            pltpu.SemaphoreType.DMA((16,)),
+            pltpu.SemaphoreType.DMA((8,)),
+            pltpu.SemaphoreType.DMA((8,)),
         ],
         compiler_params=pltpu.CompilerParams(
-            collective_id=0, has_side_effects=True, vmem_limit_bytes=48 * 1024 * 1024),
-        name="gather_product",
-    )(amplitude, pack, occ_irrep, kocc_irrep, vir_irrep.reshape(1, -1), vir_irrep)
+            collective_id=collective, has_side_effects=True, vmem_limit_bytes=56 * 1024 * 1024),
+        name="cycle_residual",
+    )(amplitude, pack, occ_irrep, kocc_irrep, vir_row, vir_irrep, *tables)
+
+
+def prepare_kernel(occ_ref, kocc_ref, lab_ref, virs_ref, w_ref, pack_ref, few_ref, *tables):
+    nk, la = w_ref.shape[0], w_ref.shape[1]
+    me = lax.axis_index("vir")
+    mine = lax.axis_index("occ")
+    mylab = virs_ref[me * la]
+    quarter = lax.broadcasted_iota(jnp.int32, (la, 640), 1) // WIN
+    for h in range(2):
+        both = []
+        for kp in range(2):
+            total = None
+            for k2 in range(2):
+                k = 4 * h + 2 * kp + k2
+                for j in range(2):
+                    want = kocc_ref[k] ^ occ_ref[2 * mine + j] ^ mylab
+                    part = jnp.where(lab_ref[...] == want, w_ref[k, :, j, :].astype(jnp.float32), 0.0)
+                    part = part + pltpu.roll(part, 2 * WIN, 1)
+                    part = part + pltpu.roll(part, WIN, 1)
+                    total = part if total is None else jnp.where(quarter >= 2 * k2 + j, part, total)
+            both.append(total)
+        pack_ref[h] = jnp.concatenate(both, axis=0).astype(jnp.bfloat16)
+
+    batch = occ_ref.shape[0]
+    occ = [occ_ref[i] for i in range(batch)]
+    blocks = [virs_ref[la * v] for v in range(16)]
+
+    def count(terms):
+        total = jnp.int32(0)
+        for t in terms:
+            total = total + t.astype(jnp.int32)
+        return total
+
+    places = [count([(occ[o] <= occ[i]) if o < i else (occ[o] < occ[i]) for o in range(batch) if o != i])
+              for i in range(batch)]
+    below = [count([occ[o] < r for o in range(batch)]) for r in range(8)] + [jnp.int32(batch)]
+    most = jnp.int32(0)
+    for r in range(8):
+        most = jnp.maximum(most, below[r + 1] - below[r])
+    few_ref[0] = most
+    for t, groups in enumerate((2, 6)):
+        order, place, begin, block_of, group_of, member_of = tables[6 * t:6 * t + 6]
+        for r in range(8):
+            begin[r] = jnp.minimum(below[r], max(batch - 3 * groups, 0))
+            for d in range(4):
+                p = jnp.int32(0)
+                for q in range(4):
+                    p = p + jnp.where(blocks[4 * q + d] == r, 4 * q + d, 0)
+                block_of[4 * r + d] = p
+        for i in range(batch):
+            place[i] = places[i]
+            slot = places[i] - begin[occ[i]]
+            group = count([slot >= 3 * q for q in range(1, groups)])
+            group_of[i] = group
+            member_of[i] = slot - 3 * group
+            order[places[i]] = i
+
+
+def prepare(occ_irrep, kocc_irrep, vir_row, vir_irrep, integral):
+    smem, vmem = pl.BlockSpec(memory_space=pltpu.SMEM), pl.BlockSpec(memory_space=pltpu.VMEM)
+    sizes = (16, 16, 8, 32, 16, 16)
+    found = pl.pallas_call(
+        prepare_kernel,
+        out_shape=[jax.ShapeDtypeStruct((2, 80, 640), jnp.bfloat16), jax.ShapeDtypeStruct((1,), jnp.int32)]
+        + [jax.ShapeDtypeStruct((n,), jnp.int32) for n in sizes + sizes],
+        in_specs=[smem, smem, vmem, smem, vmem],
+        out_specs=[vmem] + [smem] * 13,
+        name="prepare",
+    )(occ_irrep, kocc_irrep, vir_row, vir_irrep, integral)
+    return found[0], found[1], found[2:8], found[8:14]
 
 
 def shards(amplitude, integral, occ_irrep, kocc_irrep, vir_irrep):
-    vir_pos = lax.axis_index("vir")
-    occ_pos = lax.axis_index("occ")
-    local_a = amplitude.shape[1]
-    local_j = integral.shape[2]
-    n_occ = lax.axis_size("occ")
-    n_vir = lax.axis_size("vir")
-    nv = vir_irrep.shape[0]
-    own = lax.dynamic_slice_in_dim(vir_irrep, vir_pos * local_a, 1)[0]
-    j_labels = lax.dynamic_slice_in_dim(occ_irrep, occ_pos * local_j, local_j)
-    firsts = jnp.sum((vir_irrep[None, :] < jnp.arange(8)[:, None]).astype(jnp.int32), axis=1)
-    firsts = jnp.minimum(firsts, nv - WIN)
-
-    def select(labels):
-        start = jnp.sum(
-            jnp.where(labels[..., None] == jnp.arange(8), firsts, 0), axis=-1
-        )
-        b = jnp.arange(nv)[:, None]
-        n = jnp.arange(WIN)[None, :]
-        hit = (b == n + start[..., None, None]) & (vir_irrep[:, None] == labels[..., None, None])
-        return hit.astype(jnp.bfloat16)
-
-    wlab = kocc_irrep[:, None] ^ j_labels[None, :] ^ own
-    packed = jnp.einsum(
-        "kcjb,kjbn->kcjn", integral, select(wlab), preferred_element_type=jnp.float32
-    ).astype(jnp.bfloat16)
-    packed = jnp.transpose(packed.reshape(2, 2, 2, local_a, local_j * WIN), (0, 1, 3, 2, 4)).reshape(2, 2 * local_a, 640)
-    cyc = cycle_windows(amplitude, packed, occ_irrep, kocc_irrep, vir_irrep)
-    left = occ_irrep ^ own
-    batch = amplitude.shape[0]
-    cyc = cyc.reshape(batch, local_a, local_j, WIN)
-    clab = left[:, None] ^ j_labels[None, :]
-    cycle = jnp.einsum(
-        "iajn,ijbn->iajb", cyc, select(clab), preferred_element_type=jnp.float32
-    ).astype(jnp.bfloat16)
-    width = nv
-    moved = cycle.reshape(n_occ, local_j, local_a, local_j, n_vir, local_a)
-    moved = jnp.transpose(moved, (0, 4, 1, 2, 3, 5)).reshape(n_occ * n_vir * local_j, local_a, local_j, local_a)
-    moved = lax.all_to_all(moved, ("occ", "vir"), split_axis=0, concat_axis=0, tiled=True)
-    moved = moved.reshape(n_occ, n_vir, local_j, local_a, local_j, local_a)
-    mirror = jnp.transpose(moved, (0, 4, 5, 2, 1, 3)).reshape(batch, local_a, local_j, width)
-    return (cycle.astype(jnp.float32) + mirror.astype(jnp.float32)).astype(jnp.bfloat16)
+    vir_row = vir_irrep.reshape(1, -1)
+    pack, most, few_tables, all_tables = prepare(occ_irrep, kocc_irrep, vir_row, vir_irrep, integral)
+    args = (amplitude, pack, occ_irrep, kocc_irrep, vir_row, vir_irrep)
+    rows = lax.cond(
+        most[0] <= FEW,
+        lambda *a: residual_rows(2, 0, *a, *few_tables),
+        lambda *a: residual_rows(6, 1, *a, *all_tables),
+        *args,
+    )
+    return jnp.transpose(rows, (0, 2, 1, 3))
 
 
 def solution(mesh):

time: 152 us -> 59.1 us (0.39)
  local copies, waits for them, and re-layouts: 64.7 us -> 3.12 us
  blocking collectives: 34.6 us -> 0 us
  Pallas kernels: 30.3 us -> 54.7 us
  other arithmetic: 15.9 us -> 0 us
  matrix products: 5.53 us -> 0 us
    all_to_all x1 -> x0, blocking collectives: 34.6 us -> none  [shards(): lax.all_to_all(moved, ('occ', 'vir'), split_axis=0, concat_axis=0, tiled=...]
    pallas_call x1 -> x2, Pallas kernels: 30.3 us -> 54.7 us  [the longest x1 50.4 us: residual_rows(): pl.pallas_call(functools.partial(cycle_kernel, groups), out_shape=jax.Sha...]
    convert_element_type x4 -> x0, local copies, waits for them, and re-layouts: 23.9 us -> none  [the longest x2 21.2 us: shards(): mirror.astype(jnp.float32)]
    unnamed x10 -> x0, local copies, waits for them, and re-layouts: 22.2 us -> none
    reshape x5 -> x1, local copies, waits for them, and re-layouts: 15.4 us -> 0.69 us  [shards(): vir_row = vir_irrep.reshape(1, -1)]
    convert_element_type x2 -> x0, other arithmetic: 10.3 us -> none  [the longest x1 7.93 us: shards(): mirror.astype(jnp.float32)]
    dot_general x2 -> x0, matrix products: 5.53 us -> none  [the longest x1 3.56 us: shards(): jnp.einsum('iajn,ijbn->iajb', cyc, select(clab), preferred_element_type=j...]
    xor x3 -> x0, other arithmetic: 2.74 us -> none  [the longest x1 1.37 us: shards(): wlab = kocc_irrep[:, None] ^ j_labels[None, :] ^ own]
where the time goes in v3:
time: 59.1 us; the launch traced here: 58.7 us
  Pallas kernels  54.7 us (93%)
  local copies, waits for them, and re-layouts  3.12 us (5%)
  between operations  0.67 us (1%)
    pallas_call x1, Pallas kernels, residual_rows(): pl.pallas_call(functools.partial(cycle_kernel, groups), out_shape=jax.Sha...  50.4 us
    pallas_call x1, Pallas kernels, prepare(): pl.pallas_call(prepare_kernel, out_shape=[jax.ShapeDtypeStruct((2, 80, 64...  4.29 us
    cond x1, local copies, waits for them, and re-layouts, shards(): lax.cond(most[0] <= FEW, lambda *a: residual_rows(2, 0, *a, *few_tables),...  2.43 us

profile of v3, /device:TPU:1, one launch (start us, length us, event | category | flops | bytes accessed | tf_op | source)
XLA Modules:
  0.0 58.7 jit_solution(8758496880988019476)
XLA Ops:
  0.0 0.7 %reshape.7.lab_ref = s32[1,640]{1,0:T(1,128)S(1)} reshape(s32[640]{0:T(1024)} %virs_ref.1) | data formatting | bytes 5120 | tf_op jit(solution)/shard_map/reshape | solution.py:392
  0.7 4.3 %prepare.1 = (bf16[2,80,640]{2,1,0:T(8,128)(2,1)S(1)}, s32[1]{0:T(128)}, s32[16]{0:T(128)S(1)}, s32[16]{0:T(128)S(1)}, s32[8]{0:T(128)S(1)}, /*index=5*/s32[32]{...) custom-call(s32[16]{0:T(128)} %occ_ref.1, ...), custom_call_target="tpu_custom_call" | custom-call | tf_op jit(solution)/shard_map/prepare/pallas_call | solution.py:380
  5.6 50.7 %conditional.1 = (bf16[16,2,40,640]{3,2,1,0:T(8,128)(2,1)S(1)}) conditional(s32[]{:T(128)} %bitcast, (bf16[16,40,8,640]{3,2,1,0:T(8,128)(2,1)}, bf16[2,80,640]{2,1,0:T(8,128)(2,1)S(1)}, s32[16]{0:T(128)}, s32[8]{0:T(128)}, s32[1,640]{1,0:T(1,128)S(1)}, /*index=5*/s32[640]{0:T(1024)}, s32[16]{0:T(128)S(1)}, s32[16]{0:T(128)S(1)}, s32[8]{0:T(128)S(1)}, ...), branch_computations={%region_0.0_spmd, %region_1.0_spmd} | conditional | bytes 8 | solution.py:395
  5.9 50.4 %cycle_residual.3 = bf16[16,2,40,640]{3,2,1,0:T(8,128)(2,1)S(1)} custom-call(bf16[16,40,8,640]{3,2,1,0:T(8,128)(2,1)} %get-tuple-element.68.amp_ref, bf16[2,80,640]{2,1,0:T(8,128)(2,1)S(1)} %get-tuple-element.69.pack_ref, s32[16]{0:T(128)} %get-tuple-element.70.occ_ref, s32[8]{0:T(128)} %get-tuple-element.71.kocc_ref, ...), custom_call_target="tpu_custom_call" | custom-call | tf_op jit(solution)/shard_map/cond/branch_1_fun/cycle_residual/pallas_call | solution.py:280
  56.3 2.4 %copy.8 = bf16[16,2,40,640]{3,1,2,0:T(2,128)(2,1)} copy(bf16[16,2,40,640]{3,2,1,0:T(8,128)(2,1)S(1)} %get-tuple-element.108) | data formatting | bytes 3276800 | tf_op jit(solution)/shard_map/cond | solution.py:395
